TPU v7x, 128 devices: a whole 4x4x4 slice. The times are simulated.
128 devices in a mesh: layer: 2 (over core), row: 4 (over x), col: 16 (over z, y).
Axes of the slice: x: 4, y: 4, z: 4, core: 2. Of those that a mesh axis runs over, the one named last changes fastest.
Arguments:
- hamiltonian: bfloat16 [8, 16, 23, 128, 128], P(('layer', 'row'), 'col'), may hold values from -3 to 3
- cheb_low: bfloat16 [8, 16, 23, 128, 128], P(('layer', 'row'), 'col'), may hold values from -1.25 to 1.25
- cheb_high: bfloat16 [8, 16, 23, 128, 128], P(('layer', 'row'), 'col'), may hold values from -1.25 to 1.25
- pattern: int32 [2, 4, 16, 2, 23], P(None, 'row', 'col'), may hold values from -1 to 95, as said below
- atoms: int32 [768], P(('layer', 'row')), may hold values from 8 to 16
Outputs:
- cheb_even: bfloat16 [8, 16, 23, 128, 128], P(('layer', 'row'), 'col')
- cheb_odd: bfloat16 [8, 16, 23, 128, 128], P(('layer', 'row'), 'col')
Inputs may be any that keep to these rules, and one draw needn't show every extreme that they name: `pattern`: entry [q, r, g, 0, t] is a block row of the piece (below 96) and entry [q, r, g, 1, t] a block column of the group (below 48), both -1 in an empty slot. The live blocks of one piece and group are distinct, and no two of them share a block row. In every draw some piece-group pairs fill all 23 slots.
All inputs are finite; a program needn't handle non-finite values.
Results may differ from a plain program's by a relative error of at most 0.011.
Values may be sent and summed in bfloat16 or wider, within the bound.
No kernel may reach another device: no remote copies, remote signals or barrier semaphores. Data moves between devices by JAX's collectives and lax.ppermute only.
A program may use at most 192 MiB of HBM per device.

v0:
```python
import jax
import jax.numpy as jnp
from jax import lax
from jax.sharding import PartitionSpec as P

FUNCS = 8
SK = 1


def spread_2(array, axis, root):
    mine = lax.axis_index(axis) == root
    return lax.psum(jnp.where(mine, array, jnp.zeros_like(array)), axis)


def rank_in_row(row_ids):
    earlier = jnp.arange(row_ids.shape[-1], dtype=jnp.int32)
    matches = (row_ids[..., :, None] == row_ids[..., None, :]) & (
        earlier[None, :] < earlier[:, None]
    )
    return jnp.sum(matches.astype(jnp.int32), axis=-1)


def shards(hamiltonian, cheb_low, cheb_high, pattern, atoms):
    block_rows = atoms.shape[0]
    capacity = pattern.shape[-1]
    tile_size = cheb_low.shape[-1]
    grid_rows = lax.axis_size("row")
    grid_cols = lax.axis_size("col")
    layer_count = lax.axis_size("layer")
    spread = grid_cols // grid_rows
    sub_rows = block_rows // spread
    col_width = layer_count * sub_rows
    row_index = lax.axis_index("row")
    col_index = lax.axis_index("col")
    layer_index = lax.axis_index("layer")
    own_pattern = lax.dynamic_index_in_dim(pattern[:, 0, 0], layer_index, 0, keepdims=True)[:, None]
    low_panel, high_panel, index_panel = (
        lax.all_gather(cheb_low, "row", axis=0, tiled=True),
        lax.all_gather(cheb_high, "row", axis=0, tiled=True),
        lax.all_gather(own_pattern, "row", axis=0, tiled=True),
    )
    arrivals = []
    for offset in range(spread):
        arrivals.append(
            (
                spread_2(low_panel, "col", row_index * spread + offset),
                spread_2(high_panel, "col", row_index * spread + offset),
                spread_2(index_panel, "col", row_index * spread + offset),
            )
        )
    high_blocks = [arrival[1][:, 0] for arrival in arrivals]
    low_blocks = [arrival[0][:, 0] for arrival in arrivals]
    index_left = jnp.concatenate([arrival[-1] for arrival in arrivals], axis=1)
    right_rows = index_panel[:, 0, 0, :]
    right_cols = index_panel[:, 0, 1, :]
    right_live = right_rows >= 0
    right_rank = rank_in_row(right_rows)
    right_count = grid_rows * capacity
    piece_ids = jnp.arange(grid_rows, dtype=jnp.int32)[:, None]
    tile_ids = piece_ids * capacity + jnp.arange(capacity, dtype=jnp.int32)[None, :]
    safe_rows = jnp.where(right_live, right_rows, block_rows)
    right_table = jnp.full((grid_rows, block_rows, SK), right_count, jnp.int32)
    right_table = right_table.at[piece_ids, safe_rows, right_rank].set(tile_ids, mode="drop")
    right_table = right_table.reshape(grid_rows * block_rows, SK)
    right_flat = low_panel.reshape(right_count, tile_size, tile_size)
    right_cols_flat = right_cols.reshape(right_count)
    out_rows = pattern[:, 0, 0, 0, :]
    out_cols = pattern[:, 0, 0, 1, :]
    layer_ids = jnp.arange(layer_count, dtype=jnp.int32)[:, None]
    out_local = jnp.where(
        out_rows >= 0, layer_ids * block_rows + out_rows, layer_count * block_rows
    )
    slot_total = layer_count * capacity
    slot_ids = layer_ids * capacity + jnp.arange(capacity, dtype=jnp.int32)[None, :]
    slot_table = jnp.full((layer_count * block_rows, col_width), slot_total, jnp.int32)
    slot_table = slot_table.at[out_local, out_cols].set(slot_ids, mode="drop")
    left_rows = index_left[:, :, 0, :]
    left_cols = index_left[:, :, 1, :]
    left_live = left_rows >= 0
    spread_ids = jnp.arange(spread, dtype=jnp.int32)[None, :, None]
    left_piece = jnp.arange(grid_rows, dtype=jnp.int32)[:, None, None]
    inner_rows = left_piece * block_rows + jnp.clip(left_rows, 0, block_rows - 1)
    target_rows = left_cols // sub_rows * block_rows + spread_ids * sub_rows + left_cols % sub_rows
    target_rows = jnp.where(left_live, target_rows, 0)
    even_sum = jnp.zeros((slot_total, tile_size, tile_size), jnp.float32)
    odd_sum = jnp.zeros((slot_total, tile_size, tile_size), jnp.float32)
    for offset in range(spread):
        block_inner = inner_rows[:, offset].reshape(-1)
        block_target = target_rows[:, offset].reshape(-1)
        block_valid = left_live[:, offset].reshape(-1)
        low_tiles = low_blocks[offset].reshape(-1, tile_size, tile_size)
        high_tiles = high_blocks[offset].reshape(-1, tile_size, tile_size)
        picked = right_table[block_inner, 0]
        usable = block_valid & (picked < right_count)
        picked = jnp.minimum(picked, right_count - 1)
        target = jnp.where(
            usable, slot_table[block_target, jnp.maximum(right_cols_flat[picked], 0)], slot_total
        )
        right_tiles = right_flat[picked]
        even_sum = even_sum.at[target].add(
            jnp.einsum("npx,npy->nxy", low_tiles, right_tiles, preferred_element_type=jnp.float32),
            mode="drop",
        )
        odd_sum = odd_sum.at[target].add(
            jnp.einsum("npx,npy->nxy", high_tiles, right_tiles, preferred_element_type=jnp.float32),
            mode="drop",
        )
    even_total, odd_total = (
        lax.psum_scatter(
            even_sum.astype(jnp.bfloat16), "layer", scatter_dimension=0, tiled=True
        ).astype(jnp.float32),
        lax.psum_scatter(
            odd_sum.astype(jnp.bfloat16), "layer", scatter_dimension=0, tiled=True
        ).astype(jnp.float32),
    )
    own_rows = own_pattern[0, 0, 0, :]
    own_cols = own_pattern[0, 0, 1, :]
    own_live = own_rows >= 0
    global_row = (layer_index * grid_rows + row_index) * block_rows + own_rows
    global_col = (
        (own_cols // sub_rows * grid_rows + col_index // spread) * block_rows
        + col_index % spread * sub_rows
        + own_cols % sub_rows
    )
    on_diagonal = own_live & (global_row == global_col)
    functions = FUNCS * atoms[jnp.clip(own_rows, 0, block_rows - 1)]
    across = jnp.arange(tile_size, dtype=jnp.int32)
    identity = (across[:, None] == across[None, :]) & (
        across[None, None, :] < functions[:, None, None]
    )
    identity = jnp.where(on_diagonal[:, None, None] & identity, 1.0, 0.0).astype(jnp.float32)
    live_tiles = own_live[:, None, None]
    result_even = jnp.where(live_tiles, 2.0 * even_total - identity, 0.0).astype(jnp.bfloat16)
    result_odd = jnp.where(
        live_tiles, 2.0 * odd_total - hamiltonian[0, 0].astype(jnp.float32), 0.0
    ).astype(jnp.bfloat16)
    return (result_even[None, None], result_odd[None, None])


def solution(mesh):
    return jax.shard_map(
        shards,
        mesh=mesh,
        in_specs=(
            P(("layer", "row"), "col", None, None, None),
            P(("layer", "row"), "col", None, None, None),
            P(("layer", "row"), "col", None, None, None),
            P(None, "row", "col", None, None),
            P(("layer", "row")),
        ),
        out_specs=(
            P(("layer", "row"), "col", None, None, None),
            P(("layer", "row"), "col", None, None, None),
        ),
        check_vma=False,
    )
```

profile of v0, /device:TPU:1, one launch (start us, length us, event | category | flops | bytes accessed | tf_op | source)
XLA Modules:
  0.0 609.9 jit_solution(8284202051072548478)
XLA Ops:
  8.7 42.6 %all-gather.4.cloned.1.call-done = bf16[4,1,23,128,128]{4,3,2,1,0:T(8,128)(2,1)} async-done(((bf16[1,1,23,128,128]{4,3,2,1,0:T(8,128)(2,1)}), bf16[4,1,23,128,128]{4,3,2,1,0:T(8,128)(2,1)}) %all-gather.4.cloned.1.call-update) | async-done | bytes 3014672 | tf_op jit(solution)/shard_map/all_gather | solution.py:38
  51.3 40.3 %all-gather.6.cloned.1.call-done = bf16[4,1,23,128,128]{4,3,2,1,0:T(8,128)(2,1)} async-done(((bf16[1,1,23,128,128]{4,3,2,1,0:T(8,128)(2,1)}), bf16[4,1,23,128,128]{4,3,2,1,0:T(8,128)(2,1)}) %all-gather.6.cloned.1.call-update) | async-done | bytes 3014672 | tf_op jit(solution)/shard_map/all_gather | solution.py:39
  91.6 9.0 %broadcast_select_fusion = (bf16[4,1,23,128,128]{4,3,2,1,0:T(8,128)(2,1)S(1)}, bf16[4,1,23,128,128]{4,3,2,1,0:T(8,128)(2,1)}, bf16[4,1,23,128,128]{4,3,2,1,0:T(8...) fusion(bf16[4,1,23,128,128]{4,3,2,1,0:T(8,128)(2,1)} %all-gathe, ...), kind=kLoop, calls=%fused_computation.27 | loop fusion | flops 12058624 | bytes 30146564 | tf_op jit(solution)/shard_map/jit(_where)/select_n | solution.py:12
  100.7 4.6 copy.49
  105.3 4.6 copy.50
  109.9 4.7 copy.51
  114.6 4.6 copy.52
  119.2 4.6 copy.53
  123.8 4.6 copy.54
  128.4 4.6 copy.55
  136.5 5.8 all-gather
  142.3 63.5 %all-reduce.4 = (s32[4,1,2,23]{3,2,0,1:T(2,128)S(1)}, s32[4,1,2,23]{3,2,0,1:T(2,128)S(1)}, s32[4,1,2,23]{3,2,0,1:T(2,128)S(1)}, s32[4,1,2,23]{3,2,0,1:T(2,128)S(1)}) all-reduce(s32[4,1,2,23]{3,2,0,1:T(2,128)S(1)} %get-tuple-element.37, s32[4,1,2,23]{3,2,0,1:T(2,128)S(1)} %get-tuple-element.38, ...), channel_id=1, replica_groups=mesh['layer'=2,'row'=4,'col'=16] {'col'}, use_global_device_ids=true, to_apply=%region_0.1 | all-reduce | flops 736 | bytes 5888 | tf_op jit(solution)/shard_map/psum | solution.py:12
  207.8 5.0 scatter_fusion
  247.6 189.1 %all-reduce.8.cloned.1.call-done = (bf16[92,128,128]{1,2,0:T(8,128)(2,1)}, bf16[92,128,128]{1,2,0:T(8,128)(2,1)}, bf16[92,128,128]{1,2,0:T(8,128)(2,1)}, bf16[92...) async-done(((bf16[92,128,128]{1,2,0:T(8,128)(2,1)}, ...) | async-done | bytes 24117264 | tf_op jit(solution)/shard_map/psum | solution.py:12
  436.7 6.4 %fusion.66 = f32[92,128,128]{2,1,0:T(8,128)} fusion(bf16[92,128,128]{1,2,0:T(8,128)(2,1)} %get-tuple-element.6, bf16[92,128,128]{2,1,0:T(8,128)(2,1)} %gather_fusion.3), kind=kOutput, calls=%fused_computation.177 | convolution fusion | flops 385875968 | bytes 12058624 | tf_op jit(solution)/shard_map/npx,npy->nxy/dot_general | solution.py:101
  443.1 3.9 fusion.67
  447.9 3.9 fusion.68
  452.7 3.5 fusion.69
  456.6 12.8 %scatter_fusion.2 = f32[46,128,128]{2,1,0:T(8,128)S(1)} fusion(f32[46,128,128]{2,1,0:T(8,128)S(1)} %broadcast.723.clone.1, s32[92]{0:T(128)S(1)} %fusion.30, f32[92,128,128]{2,1,0:T(8,128)} %fusion.66), kind=kCustom, calls=%fused_computation.19 | custom fusion | flops 1507328 | bytes 18088304 | tf_op jit(solution)/shard_map/scatter-add | solution.py:100
  469.4 12.8 %scatter_fusion.3 = f32[46,128,128]{2,1,0:T(8,128)S(1)} fusion(f32[46,128,128]{2,1,0:T(8,128)S(1)} %scatter_fusion.2, s32[92]{0:T(128)S(1)} %fusion.38, f32[92,128,128]{2,1,0:T(8,128)} %fusion.67), kind=kCustom, calls=%fused_computation.20 | custom fusion | flops 1507328 | bytes 18088304 | tf_op jit(solution)/shard_map/scatter-add | solution.py:100
  482.2 12.8 %scatter_fusion.4 = f32[46,128,128]{2,1,0:T(8,128)S(1)} fusion(f32[46,128,128]{2,1,0:T(8,128)S(1)} %scatter_fusion.3, s32[92]{0:T(128)S(1)} %fusion.46, f32[92,128,128]{2,1,0:T(8,128)} %fusion.68), kind=kCustom, calls=%fused_computation.21 | custom fusion | flops 1507328 | bytes 18088304 | tf_op jit(solution)/shard_map/scatter-add | solution.py:100
  495.0 12.8 %scatter_fusion.5 = f32[46,128,128]{2,1,0:T(8,128)S(1)} fusion(f32[46,128,128]{2,1,0:T(8,128)S(1)} %scatter_fusion.4, s32[92]{0:T(128)S(1)} %fusion.54, f32[92,128,128]{2,1,0:T(8,128)} %fusion.69), kind=kCustom, calls=%fused_computation.22 | custom fusion | flops 1507328 | bytes 18088304 | tf_op jit(solution)/shard_map/scatter-add | solution.py:100
  509.3 6.3 %fusion.70 = f32[92,128,128]{2,1,0:T(8,128)} fusion(bf16[92,128,128]{1,2,0:T(8,128)(2,1)} %get-tuple-element.10, bf16[92,128,128]{2,1,0:T(8,128)(2,1)} %gather_fusion.3), kind=kOutput, calls=%fused_computation.181 | convolution fusion | flops 385875968 | bytes 12058624 | tf_op jit(solution)/shard_map/npx,npy->nxy/dot_general | solution.py:105
  515.9 13.1 %scatter_fusion.6 = f32[46,128,128]{2,1,0:T(8,128)S(1)} fusion(f32[46,128,128]{2,1,0:T(8,128)S(1)} %broadcast.723.clone, s32[92]{0:T(128)S(1)} %fusion.30, f32[92,128,128]{2,1,0:T(8,128)} %fusion.70), kind=kCustom, calls=%fused_computation.23 | custom fusion | flops 1507328 | bytes 18088304 | tf_op jit(solution)/shard_map/scatter-add | solution.py:104
  529.0 6.3 %fusion.71 = f32[92,128,128]{2,1,0:T(8,128)} fusion(bf16[92,128,128]{1,2,0:T(8,128)(2,1)} %get-tuple-element.11, bf16[92,128,128]{2,1,0:T(8,128)(2,1)} %gather_fusion.7), kind=kOutput, calls=%fused_computation.182 | convolution fusion | flops 385875968 | bytes 12058624 | tf_op jit(solution)/shard_map/npx,npy->nxy/dot_general | solution.py:105
  535.3 12.8 %scatter_fusion.7 = f32[46,128,128]{2,1,0:T(8,128)S(1)} fusion(f32[46,128,128]{2,1,0:T(8,128)S(1)} %scatter_fusion.6, s32[92]{0:T(128)S(1)} %fusion.38, f32[92,128,128]{2,1,0:T(8,128)} %fusion.71), kind=kCustom, calls=%fused_computation.24 | custom fusion | flops 1507328 | bytes 18088304 | tf_op jit(solution)/shard_map/scatter-add | solution.py:104
  548.1 6.3 %fusion.72 = f32[92,128,128]{2,1,0:T(8,128)} fusion(bf16[92,128,128]{1,2,0:T(8,128)(2,1)} %get-tuple-element.12, bf16[92,128,128]{2,1,0:T(8,128)(2,1)} %gather_fusion.11), kind=kOutput, calls=%fused_computation.183 | convolution fusion | flops 385875968 | bytes 12058624 | tf_op jit(solution)/shard_map/npx,npy->nxy/dot_general | solution.py:105
  554.4 12.8 %scatter_fusion.8 = f32[46,128,128]{2,1,0:T(8,128)S(1)} fusion(f32[46,128,128]{2,1,0:T(8,128)S(1)} %scatter_fusion.7, s32[92]{0:T(128)S(1)} %fusion.46, f32[92,128,128]{2,1,0:T(8,128)} %fusion.72), kind=kCustom, calls=%fused_computation.25 | custom fusion | flops 1507328 | bytes 18088304 | tf_op jit(solution)/shard_map/scatter-add | solution.py:104
  567.2 6.3 %fusion.73 = f32[92,128,128]{2,1,0:T(8,128)} fusion(bf16[92,128,128]{1,2,0:T(8,128)(2,1)} %get-tuple-element.13, bf16[92,128,128]{2,1,0:T(8,128)(2,1)} %gather_fusion.15), kind=kOutput, calls=%fused_computation.184 | convolution fusion | flops 385875968 | bytes 12058624 | tf_op jit(solution)/shard_map/npx,npy->nxy/dot_general | solution.py:105
  573.5 12.8 %scatter_fusion.9 = f32[46,128,128]{2,1,0:T(8,128)S(1)} fusion(f32[46,128,128]{2,1,0:T(8,128)S(1)} %scatter_fusion.8, s32[92]{0:T(128)S(1)} %fusion.54, f32[92,128,128]{2,1,0:T(8,128)} %fusion.73), kind=kCustom, calls=%fused_computation.26 | custom fusion | flops 1507328 | bytes 18088304 | tf_op jit(solution)/shard_map/scatter-add | solution.py:104
  588.6 11.3 %reduce-scatter.5.cloned.1.call-done = bf16[23,128,128]{2,1,0:T(8,128)(2,1)} async-done(((bf16[46,128,128]{2,1,0:T(8,128)(2,1)}), bf16[23,128,128]{2,1,0:T(8,128)(2,1)}) %reduce-scatter.5.cloned.1.call-update) | async-done | bytes 753680 | tf_op jit(solution)/shard_map/reduce_scatter | solution.py:112
  599.9 3.5 fusion.3
  (126 shorter events, 47.6 us)
Async XLA Ops:
  7.2 580.6 %copy-start = (s32[96]{0:T(128)S(1)}, s32[96]{0:T(128)}, u32[]{:S(2)}) copy-start(s32[96]{0:T(128)} %param.9) | copy-start | bytes 1156
  7.2 44.2 %all-gather.4.cloned.1.call-start = ((), (), s32[]{:S(2)}) async-start(), calls=%async_computation.2 | async-start | bytes 3768320 | tf_op jit(solution)/shard_map/all_gather | solution.py:38
  7.9 83.7 %all-gather.6.cloned.1.call-start = ((), (), s32[]{:S(2)}) async-start(), calls=%async_computation.4 | async-start | bytes 3768320 | tf_op jit(solution)/shard_map/all_gather | solution.py:39
  8.7 428.0 %all-reduce.8.cloned.1.call-start = ((), (), s32[]{:S(2)}) async-start(), calls=%async_computation.6 | async-start | bytes 48234496 | tf_op jit(solution)/shard_map/psum | solution.py:12
  135.8 0.7 copy-start.8
  135.9 452.7 %reduce-scatter.3.cloned.1.call-start = ((), (), s32[]{:S(2)}) async-start(), calls=%async_computation.3 | async-start | bytes 2260992 | tf_op jit(solution)/shard_map/reduce_scatter | solution.py:109
  219.2 17.8 %copy-start.1 = (bf16[4,1,23,128,128]{4,3,2,1,0:T(8,128)(2,1)S(1)}, bf16[4,1,23,128,128]{4,3,2,1,0:T(8,128)(2,1)}, u32[]{:S(2)}) copy-start(bf16[4,1,23,128,128]{4,3,2,1,0:T(8,128)(2,1)} %all-gather.4.cloned.1.call-done) | copy-start | bytes 9043972
  436.7 6.4 %copy-start.4 = (bf16[92,128,128]{2,1,0:T(8,128)(2,1)S(1)}, bf16[92,128,128]{2,1,0:T(8,128)(2,1)}, u32[]{:S(2)}) copy-start(bf16[92,128,128]{2,1,0:T(8,128)(2,1)} %gather_fusion.7) | copy-start | bytes 9043972
  436.7 6.4 %copy-start.7 = (bf16[92,128,128]{1,2,0:T(8,128)(2,1)S(1)}, bf16[92,128,128]{1,2,0:T(8,128)(2,1)}, u32[]{:S(2)}) copy-start(bf16[92,128,128]{1,2,0:T(8,128)(2,1)} %get-tuple-element.7) | copy-start | bytes 9043972
  443.1 4.0 copy-start.3
  443.1 4.8 copy-start.6
  447.9 4.0 copy-start.2
  447.9 4.8 copy-start.5
  509.2 90.6 %reduce-scatter.5.cloned.1.call-start = ((), (), s32[]{:S(2)}) async-start(), calls=%async_computation.5 | async-start | bytes 2260992 | tf_op jit(solution)/shard_map/reduce_scatter | solution.py:112
Sparse Core Ops, SparseCore 0:
  9.7 41.6 all-gather.3
  53.0 38.5 all-gather.5
  136.0 300.6 all-reduce.7
  509.3 11.7 reduce-scatter.2
  587.8 12.0 reduce-scatter.4
where the time goes:
time: 613 us; the launch traced here: 610 us
  waiting for transfers between devices  285 us (46%)
  other arithmetic  120 us (20%)
  local copies, waits for them, and re-layouts  78.7 us (13%)
  blocking collectives  69.3 us (11%)
  matrix products  42.9 us (7%)
  between operations  14.3 us (2%)
    psum x1, waiting for transfers between devices, spread_2(): return lax.psum(jnp.where(mine, array, jnp.zeros_like(array)), axis)  189 us
    psum x1, blocking collectives, spread_2(): return lax.psum(jnp.where(mine, array, jnp.zeros_like(array)), axis)  63.5 us
    scatter-add x4, other arithmetic, shards(): odd_sum.at[target]  51.5 us
    scatter-add x4, other arithmetic, shards(): even_sum.at[target]  51.2 us
    all_gather x1, waiting for transfers between devices, shards(): lax.all_gather(cheb_low, 'row', axis=0, tiled=True)  42.6 us
    all_gather x1, waiting for transfers between devices, shards(): lax.all_gather(cheb_high, 'row', axis=0, tiled=True)  40.3 us
    select_n x8, local copies, waits for them, and re-layouts, spread_2(): return lax.psum(jnp.where(mine, array, jnp.zeros_like(array)), axis)  35.1 us
    dot_general x4, matrix products, shards(): jnp.einsum('npx,npy->nxy', high_tiles, right_tiles, preferred_element_typ...  25.1 us
  transfers between devices with their start and end apart: 5, of which 4 were waited for; matrix products, arithmetic and copies ran while one was open for 20% of the time, Pallas kernels for 0%

commit v1 on v0

--- a/solution.py
+++ b/solution.py
@@ -1,10 +1,488 @@
+import functools
+
 import jax
 import jax.numpy as jnp
 from jax import lax
+from jax.experimental import pallas as pl
+from jax.experimental.pallas import tpu as pltpu
 from jax.sharding import PartitionSpec as P
 
 FUNCS = 8
 SK = 1
+TILE = 128
+CAP = 23
+RB = 96
+LANES = 32
+SPAN = 4
+HALF = 12
+LIST = 9
+EXTRA = 2
+BLOB = 2 * TILE + 16
+BF = jnp.bfloat16
+F32 = jnp.float32
+I32 = jnp.int32
+VM = pl.BlockSpec(memory_space=pltpu.VMEM)
+SM = pl.BlockSpec(memory_space=pltpu.SMEM)
+LIMIT = 56 * 1024 * 1024
+
+
+def to_column(row, n):
+    eye = lax.broadcasted_iota(I32, (n, n), 0) == lax.broadcasted_iota(I32, (n, n), 1)
+    return jnp.sum(jnp.where(eye, row, 0.0), axis=1, keepdims=True)
+
+
+def one(cond):
+    return jnp.where(cond, 1.0, 0.0)
+
+
+def piece_row(patterns, index, layer):
+    both = patterns[pl.ds(index, 1), :]
+    here = jnp.where(layer == 0, both[:, : 2 * LANES], both[:, 2 * LANES :])
+    return here[:, :LANES], here[:, LANES:]
+
+
+def positions(needed):
+    rows = lax.broadcasted_iota(I32, (LANES, LANES), 0)
+    lanes = lax.broadcasted_iota(I32, (LANES, LANES), 1)
+    as_row = jnp.sum(jnp.where(rows == lanes, needed, 0.0), axis=0, keepdims=True)
+    return jnp.sum(jnp.where(lanes < rows, as_row, 0.0), axis=1, keepdims=True)
+
+
+def meta_block(fields):
+    lanes = lax.broadcasted_iota(I32, (16, TILE), 1)
+    block = jnp.zeros((16, TILE), F32)
+    for i, value in enumerate(fields):
+        block = jnp.where(lanes == i, value.astype(F32), block)
+    return block.astype(BF)
+
+
+BITS = (0, 1, 3, 5, 12, 13, 18, 20)
+WIDE = (1, 2, 2, 7, 1, 5, 2, 1)
+
+
+def read_meta(block):
+    lanes = lax.broadcasted_iota(I32, (16, TILE), 1)
+    weights = jnp.zeros((16, TILE), F32)
+    for i, bit in enumerate(BITS):
+        weights = jnp.where(lanes == i, float(1 << bit), weights)
+    code = jnp.max(jnp.sum(block.astype(F32) * weights, axis=1, keepdims=True)).astype(I32)
+    return [(code >> bit) & ((1 << wide) - 1) for bit, wide in zip(BITS, WIDE)]
+
+
+def plan_kernel(where, own, patterns, low, high, table, extra):
+    q, r, z, y = where[0], where[1], where[2], where[3]
+    g = z * SPAN + y
+    me = r * 16 + g
+    own_k, own_j = piece_row(patterns, me, q)
+    k_col, j_col = to_column(own_k, LANES), to_column(own_j, LANES)
+    lanes = lax.broadcasted_iota(I32, (LANES, LANES), 1)
+    slot_col = lax.broadcasted_iota(I32, (LANES, 1), 0).astype(F32)
+
+    def center(s):
+        ck, cj = piece_row(patterns, r * 20 + s, q)
+        ck = jnp.where((ck >= 0) & (ck == cj), ck, -2.0)
+        return to_column(ck, LANES)
+
+    def needed_by(center_col, line_y):
+        lk, lj = piece_row(patterns, r * 16 + z * SPAN + line_y, q)
+        lk = jnp.where(lk == lj, -1.0, lk)
+        return jnp.max(one(center_col == lk), axis=1, keepdims=True)
+
+    table[...] = jnp.zeros_like(table)
+    overflow = jnp.zeros((1, 1), F32)
+    mine = center(y)
+    for d in range(1, SPAN):
+        needed = needed_by(mine, (y + d) % SPAN)
+        pos = positions(needed)
+        chosen = (needed > 0) & (pos.astype(I32) == lanes)
+        entries = jnp.sum(jnp.where(chosen, slot_col, 0.0), axis=0, keepdims=True)
+        table[d - 1 : d, :LANES] = entries.astype(I32)
+        total = jnp.sum(needed, axis=0, keepdims=True)
+        overflow = jnp.maximum(overflow, one(total > LIST))
+    code = jnp.zeros((1, LANES), F32)
+    own_off = jnp.where(own_k == own_j, -1.0, own_k)
+    for d in range(SPAN):
+        there = center((y + SPAN - d) % SPAN)
+        needed = needed_by(there, y)
+        if d:
+            entry = 1.0 + LANES * d + positions(needed)
+        else:
+            entry = 1.0 + slot_col
+        code = code + jnp.sum(jnp.where(there == own_off, entry, 0.0), axis=0, keepdims=True)
+    table[3:4, :LANES] = code.astype(I32)
+
+    outs = []
+    for layer in range(2):
+        ok, oj = piece_row(patterns, z * 16 + g, layer)
+        outs.append(to_column(jnp.where(ok == oj, ok, -2.0), LANES))
+    for i, step in enumerate((0, 1, 3, 2)):
+        _, sj = piece_row(patterns, ((z + step) % SPAN) * 16 + g, q)
+        target = jnp.zeros((1, LANES), F32)
+        for layer in range(2):
+            hit = (outs[layer] == sj) & (sj >= 0)
+            target = target + jnp.sum(
+                jnp.where(hit, 1.0 + LANES * layer + slot_col, 0.0), axis=0, keepdims=True
+            )
+        target = jnp.where(r == z, target, 0.0)
+        table[4 + i : 5 + i, :LANES] = target.astype(I32)
+
+    wide = lax.broadcasted_iota(I32, (LANES, 2 * LANES), 1)
+    deep = lax.broadcasted_iota(I32, (LANES, 2 * LANES), 0)
+    first = jnp.zeros((LANES, 2 * LANES), F32)
+    second = jnp.zeros((LANES, 2 * LANES), F32)
+    lefts = jnp.zeros((LANES, 2 * LANES), F32)
+    rights = jnp.zeros((LANES, 2 * LANES), F32)
+
+    def out_rows(row):
+        ks = jnp.concatenate([row[:, :LANES], row[:, 2 * LANES : 3 * LANES]], axis=1)
+        js = jnp.concatenate([row[:, LANES : 2 * LANES], row[:, 3 * LANES :]], axis=1)
+        return ks, js
+
+    for other in range(16):
+        uk, uj = piece_row(patterns, r * 16 + other, q)
+        partner = jnp.sum(jnp.where((k_col == uk) & (uk >= 0), uj + 1.0, 0.0), axis=1, keepdims=True) - 1.0
+        vk, vj = out_rows(patterns[pl.ds(z * 16 + other, 1), :])
+        hit = (partner == vj) & (vk == j_col) & (vk >= 0)
+        hit = hit & (partner != j_col) & (j_col != k_col)
+        lefts = lefts + one(hit)
+        entry = jnp.where(hit, (1 + deep + LANES * wide + 2048 * other).astype(F32), 0.0)
+        second = jnp.maximum(second, jnp.minimum(first, entry))
+        first = jnp.maximum(first, entry)
+        wk, wj = out_rows(patterns[pl.ds((other // SPAN) * 16 + g, 1), :])
+        hit = (partner == wk) & (wj == j_col) & (wj >= 0)
+        hit = hit & (partner != j_col) & (partner != k_col)
+        rights = rights + one(hit)
+    many = jnp.maximum(one(jnp.sum(lefts) > EXTRA), one(jnp.sum(rights) > EXTRA))
+    flag = jnp.maximum(jnp.max(overflow), many)
+    top = jnp.max(first)
+    next_top = jnp.maximum(jnp.max(jnp.where(first == top, 0.0, first)), jnp.max(second))
+    for i, best in enumerate((top, next_top)):
+        entry = best.astype(I32)
+        valid = jnp.minimum(entry, 1)
+        entry = jnp.maximum(entry - 1, 0)
+        left = entry % LANES
+        out = (entry // LANES) % (2 * LANES)
+        to = entry // 2048
+        left = jnp.minimum(left, CAP - 1)
+        row = jnp.maximum(own[2 * q, left], 0)
+        extra[i, :TILE, :] = low[left]
+        extra[i, TILE : 2 * TILE, :] = high[left]
+        extra[i, 2 * TILE :, :] = meta_block(
+            (valid, to // SPAN, to % SPAN, row, out // LANES, out % LANES, z, flag)
+        )
+
+
+def pack_kernel(where, table, own, p1, p2, p3, p4, b1, b2, b3):
+    kind = (where[1] - where[2] + SPAN) % SPAN
+    for d, buffer in enumerate((b1, b2, b3)):
+
+        def step(j, _, d=d, buffer=buffer):
+            m = jnp.minimum(table[d, j], CAP - 1)
+            copy_left(kind, m, own, p1, p2, p3, p4, buffer, j)
+            return 0
+
+        lax.fori_loop(0, LIST, step, 0)
+
+
+def copy_left(kind, m, own, p1, p2, p3, p4, buffer, j):
+    @pl.when(kind == 0)
+    def _():
+        buffer[j] = own[m]
+
+    @pl.when(kind == 3)
+    def _():
+        buffer[j] = p1[m]
+
+    @pl.when(kind == 1)
+    def _():
+        buffer[j] = p2[m]
+
+    @pl.when((kind == 2) & (m < HALF))
+    def _():
+        buffer[j] = p3[jnp.minimum(m, HALF - 1)]
+
+    @pl.when((kind == 2) & (m >= HALF))
+    def _():
+        buffer[j] = p4[jnp.maximum(m - HALF, 0)]
+
+
+def forward_kernel(where, e0, e1, e2, e3, b0, b1, b2, b3):
+    z, y = where[2], where[3]
+    metas = [read_meta(e[i, 2 * TILE :, :]) for e in (e0, e1, e2, e3) for i in range(EXTRA)]
+    flag = functools.reduce(jnp.maximum, [m[7] for m in metas])
+    zero = jnp.int32(0)
+    for d, buffer in enumerate((b0, b1, b2, b3)):
+        for i in range(EXTRA):
+            buffer[i] = jnp.zeros((BLOB, TILE), BF)
+            buffer[i, 2 * TILE :, :] = meta_block((zero,) * 7 + (flag,))
+        count = jnp.int32(0)
+        for n, e in enumerate((e0, e1, e2, e3)):
+            for i in range(EXTRA):
+                m = metas[n * EXTRA + i]
+                take = (m[0] > 0) & (m[1] == z) & (m[2] == (y + d) % SPAN)
+
+                @pl.when(take & (count < EXTRA))
+                def _(buffer=buffer, e=e, i=i, m=m, count=count):
+                    buffer[count, : 2 * TILE, :] = e[i, : 2 * TILE, :]
+                    buffer[count, 2 * TILE :, :] = meta_block((*m[:7], flag))
+
+                count = count + take.astype(I32)
+
+
+def contract(left, right):
+    return lax.dot_general(left, right, (((0,), (0,)), ((), ())), preferred_element_type=F32)
+
+
+def extra_kernel(where, own, low, e0, e1, e2, e3, result):
+    q = where[0]
+    metas = [read_meta(e[i, 2 * TILE :, :]) for e in (e0, e1, e2, e3) for i in range(EXTRA)]
+    flag = functools.reduce(jnp.maximum, [m[7] for m in metas])
+    zero = jnp.int32(0)
+    for i in range(EXTRA):
+        result[i] = jnp.zeros((BLOB, TILE), BF)
+        result[i, 2 * TILE :, :] = meta_block((zero,) * 7 + (flag,))
+    count = jnp.int32(0)
+    for n, e in enumerate((e0, e1, e2, e3)):
+        for i in range(EXTRA):
+            m = metas[n * EXTRA + i]
+            take = m[0] > 0
+
+            @pl.when(take & (count < EXTRA))
+            def _(e=e, i=i, m=m, count=count):
+                def find(t, at):
+                    return jnp.where(own[2 * q, t] == m[3], t, at)
+
+                right = low[lax.fori_loop(0, CAP, find, jnp.int32(0))]
+                for half in range(2):
+                    rows = slice(half * TILE, (half + 1) * TILE)
+                    result[count, rows, :] = contract(e[i, rows, :], right).astype(BF)
+                result[count, 2 * TILE :, :] = meta_block((*m[:7], flag))
+
+            count = count + take.astype(I32)
+
+
+def self_kernel(where, table, own, p1, p2, p3, p4, rown, r1, r2, r3, r4, mine, theirs, sums):
+    q = where[0]
+
+    @pl.when(where[1] == where[2])
+    def _():
+        sums[...] = jnp.zeros_like(sums)
+
+        def step(i, left, right, offset):
+            def body(t, _):
+                target = table[i, t + offset]
+
+                @pl.when(target > 0)
+                def _():
+                    sums[target - 1] += contract(left[t], right[t])
+
+                return 0
+
+            lax.fori_loop(0, left.shape[0], body, 0)
+
+        step(4, own, rown, 0)
+        step(5, p1, r1, 0)
+        step(6, p2, r2, 0)
+        step(7, p3, r3, 0)
+        step(7, p4, r4, HALF)
+        for t in range(CAP):
+            mine[t] = sums[q * LANES + t]
+            theirs[t] = sums[(1 - q) * LANES + t].astype(BF)
+
+
+def final_kernel(odd, where, own, atoms, table, low, left, p1, p2, p3, p4, b1, b2, b3,
+                 mine, theirs, here, there, ham, out, total, tile):
+    q, r, z, y = where[0], where[1], where[2], where[3]
+    kind = (r - z + SPAN) % SPAN
+
+    @pl.when(kind == 0)
+    def _():
+        def body(t, _):
+            total[t] = mine[t] + theirs[t].astype(F32)
+            return 0
+
+        lax.fori_loop(0, CAP, body, 0)
+
+    @pl.when(kind != 0)
+    def _():
+        total[...] = jnp.zeros_like(total)
+
+    def product(t, _):
+        code = table[3, t] - 1
+
+        @pl.when(code >= 0)
+        def _():
+            d, m = code // LANES, jnp.minimum(code % LANES, CAP - 1)
+
+            @pl.when(d == 0)
+            def _():
+                copy_left(kind, m, left, p1, p2, p3, p4, tile, 0)
+
+            for i, buffer in enumerate((b1, b2, b3)):
+
+                @pl.when(d == i + 1)
+                def _(buffer=buffer):
+                    tile[0] = buffer[jnp.minimum(m, LIST - 1)]
+
+            total[t] += contract(tile[0], low[t])
+
+        return 0
+
+    lax.fori_loop(0, CAP, product, 0)
+    for e in (here, there):
+        for i in range(SPAN * EXTRA):
+            m = read_meta(e[i, 2 * TILE :, :])
+
+            @pl.when((m[0] > 0) & (m[4] == q) & (m[6] == r))
+            def _(e=e, i=i, m=m):
+                rows = slice(odd * TILE, (odd + 1) * TILE)
+                slot = jnp.minimum(m[5], CAP - 1)
+                total[slot] += e[i, rows, :].astype(F32)
+
+    rows = lax.broadcasted_iota(I32, (TILE, TILE), 0)
+    lanes = lax.broadcasted_iota(I32, (TILE, TILE), 1)
+    diagonal = rows == lanes
+
+    def finish(t, _):
+        a, b = own[2 * q, t], own[2 * q + 1, t]
+
+        @pl.when(a >= 0)
+        def _():
+            if odd:
+                taken = ham[t].astype(F32)
+            else:
+                col = (b // 24 * SPAN + z) * RB + y * 24 + b % 24
+                on = (q * SPAN + r) * RB + a == col
+                functions = jnp.where(on, FUNCS * atoms[a], 0)
+                taken = one(diagonal & (lanes < functions))
+            out[t] = (2.0 * total[t] - taken).astype(BF)
+
+        @pl.when(a < 0)
+        def _():
+            out[t] = jnp.zeros((TILE, TILE), BF)
+
+        return 0
+
+    lax.fori_loop(0, CAP, finish, 0)
+
+
+def flag_kernel(here, there, flag):
+    worst = jnp.int32(0)
+    for e in (here, there):
+        for i in range(0, SPAN * EXTRA, EXTRA):
+            worst = jnp.maximum(worst, read_meta(e[i, 2 * TILE :, :])[7])
+    flag[0, 0] = worst
+
+
+def call(kernel, outs, ins, out_specs=None, scratch=(), name=None):
+    return pl.pallas_call(
+        kernel,
+        out_shape=outs,
+        in_specs=ins,
+        out_specs=out_specs if out_specs is not None else jax.tree.map(lambda _: VM, outs),
+        scratch_shapes=list(scratch),
+        compiler_params=pltpu.CompilerParams(vmem_limit_bytes=LIMIT),
+        name=name,
+    )
+
+
+def plane(move):
+    pairs = []
+    for x in range(SPAN):
+        for z in range(SPAN):
+            to = move((x - z) % SPAN, x, z)
+            if to is not None:
+                for y in range(SPAN):
+                    pairs.append(((x * SPAN + z) * SPAN + y, ((to[0] % SPAN) * SPAN + to[1] % SPAN) * SPAN + y))
+    return pairs
+
+
+STEP1 = plane(lambda k, x, z: {0: (x, z + 1), 1: (z, z), 2: (z + 1, z)}.get(k))
+STEP2 = plane(lambda k, x, z: {0: (x, z - 1), 3: (z, z), 2: (z - 1, z)}.get(k))
+STEP3 = plane(lambda k, x, z: {3: (x, z + 1), 1: (z, z)}.get(k))
+STEP4 = plane(lambda k, x, z: {1: (x, z - 1), 3: (z, z)}.get(k))
+
+
+def along_z(d):
+    return [(z * SPAN + y, (z + d) % SPAN * SPAN + y) for z in range(SPAN) for y in range(SPAN)]
+
+
+def along_y(d):
+    return [(z * SPAN + y, z * SPAN + (y + d) % SPAN) for z in range(SPAN) for y in range(SPAN)]
+
+
+def along_x(d):
+    return [(x, (x + d) % SPAN) for x in range(SPAN)]
+
+
+def spread_tiles(tiles):
+    axes = ("row", "col")
+    p1 = lax.ppermute(tiles, axes, STEP1)
+    p2 = lax.ppermute(tiles, axes, STEP2)
+    p3 = lax.ppermute(p1[:HALF], axes, STEP3)
+    p4 = lax.ppermute(p2[HALF:], axes, STEP4)
+    return p1, p2, p3, p4
+
+
+def sparse(hamiltonian, cheb_low, cheb_high, pattern, atoms):
+    shape = jax.ShapeDtypeStruct
+    tiles = (CAP, TILE, TILE)
+    low = cheb_low.reshape(tiles)
+    high = cheb_high.reshape(tiles)
+    ham = hamiltonian.reshape(tiles)
+    layer, x, col = (lax.axis_index(a) for a in ("layer", "row", "col"))
+    where = jnp.stack([layer, x, col // SPAN, col % SPAN]).astype(I32)
+    own = pattern.reshape(4, CAP)
+    a, b = pattern[:, 0, 0, 0, :], pattern[:, 0, 0, 1, :]
+    k = (jnp.arange(2, dtype=I32)[:, None] * SPAN + x) * RB + a
+    j = (b // 24 * SPAN + col // SPAN) * RB + col % SPAN * 24 + b % 24
+    live = (a >= 0)[:, None, :]
+    named = jnp.where(live, jnp.stack([k, j], axis=1), -1).astype(F32)
+    named = jnp.pad(named, ((0, 0), (0, 0), (0, LANES - CAP)), constant_values=-1.0)
+    named = jnp.broadcast_to(named.reshape(1, 4 * LANES), (64, 4 * LANES))
+    lows = spread_tiles(low)
+    patterns = lax.all_to_all(named, ("row", "col"), 0, 0, tiled=True)
+    highs = spread_tiles(high)
+
+    blob = shape((EXTRA, BLOB, TILE), BF)
+    table, extra = call(
+        plan_kernel, (shape((8, TILE), I32), blob), [SM, SM, VM, VM, VM], name="plan"
+    )(where, own, patterns, low, high)
+    arrived = [lax.ppermute(extra, "col", along_z(d)) for d in (1, 2, 3)]
+    forward = call(forward_kernel, (blob,) * 4, [SM] + [VM] * 4, name="forward")(where, extra, *arrived)
+    arrived = [lax.ppermute(forward[d], "col", along_y(d)) for d in (1, 2, 3)]
+    result = call(extra_kernel, blob, [SM, SM] + [VM] * 5, name="extra")(
+        where, own, low, forward[0], *arrived
+    )
+    here = jnp.concatenate([result] + [lax.ppermute(result, "row", along_x(d)) for d in (1, 2, 3)])
+    there = lax.ppermute(here, "layer", [(0, 1), (1, 0)])
+    flag = call(flag_kernel, shape((1, 1), I32), [VM, VM], out_specs=SM, name="flag")(here, there)
+
+    lists = shape((LIST, TILE, TILE), BF)
+    results = []
+    for odd, (left, spread) in enumerate(((low, lows), (high, highs))):
+        packed = call(pack_kernel, (lists,) * 3, [SM, SM] + [VM] * 5, name="pack")(
+            where, table, left, *spread
+        )
+        lines = [lax.ppermute(packed[d - 1], "col", along_y(d)) for d in (1, 2, 3)]
+        mine, theirs = call(
+            self_kernel,
+            (shape(tiles, F32), shape(tiles, BF)),
+            [SM, SM] + [VM] * 10,
+            scratch=[pltpu.VMEM((2 * LANES, TILE, TILE), F32)],
+            name="squares",
+        )(where, table, left, *spread, low, *lows)
+        theirs = lax.ppermute(theirs, "layer", [(0, 1), (1, 0)])
+        results.append(
+            call(
+                functools.partial(final_kernel, odd),
+                shape(tiles, BF),
+                [SM] * 4 + [VM] * 14,
+                scratch=[pltpu.VMEM(tiles, F32), pltpu.VMEM((1, TILE, TILE), BF)],
+                name="finish",
+            )(where, own, atoms, table, low, left, *spread, *lines, mine, theirs, here, there, ham)
+        )
+    return flag, [out[None, None] for out in results]
 
 
 def spread_2(array, axis, root):
@@ -20,7 +498,7 @@
     return jnp.sum(matches.astype(jnp.int32), axis=-1)
 
 
-def shards(hamiltonian, cheb_low, cheb_high, pattern, atoms):
+def panels(hamiltonian, cheb_low, cheb_high, pattern, atoms):
     block_rows = atoms.shape[0]
     capacity = pattern.shape[-1]
     tile_size = cheb_low.shape[-1]
@@ -137,6 +615,15 @@
     return (result_even[None, None], result_odd[None, None])
 
 
+def shards(hamiltonian, cheb_low, cheb_high, pattern, atoms):
+    flag, (even, odd) = sparse(hamiltonian, cheb_low, cheb_high, pattern, atoms)
+    return lax.cond(
+        flag[0, 0] > 0,
+        lambda: panels(hamiltonian, cheb_low, cheb_high, pattern, atoms),
+        lambda: (even, odd),
+    )
+
+
 def solution(mesh):
     return jax.shard_map(
         shards,

time: 613 us -> 218 us (0.36)
  waiting for transfers between devices: 285 us -> 66.5 us
  other arithmetic: 120 us -> 3.26 us
  local copies, waits for them, and re-layouts: 78.7 us -> 6.65 us
  blocking collectives: 69.3 us -> 0 us
  starting transfers between devices: 0.2 us -> 62.8 us
  Pallas kernels: 0 us -> 61.3 us
  matrix products: 42.9 us -> 0 us
    psum x1 -> x0, waiting for transfers between devices: 189 us -> none  [spread_2(): return lax.psum(jnp.where(mine, array, jnp.zeros_like(array)), axis)]
    scatter-add x8 -> x0, other arithmetic: 103 us -> none  [the longest x4 51.5 us: shards(): odd_sum.at[target]]
    all_gather x2 -> x0, waiting for transfers between devices: 82.9 us -> none  [the longest x1 42.6 us: shards(): lax.all_gather(cheb_low, 'row', axis=0, tiled=True)]
    psum x1 -> x0, blocking collectives: 63.5 us -> none  [spread_2(): return lax.psum(jnp.where(mine, array, jnp.zeros_like(array)), axis)]
    pallas_call x0 -> x10, Pallas kernels: none -> 61.3 us  [the longest x2 29.6 us: sparse(): call(self_kernel, (shape(tiles, F32), shape(tiles, BF)), [SM, SM] + [VM]...]
    ppermute x0 -> x26, starting transfers between devices: none -> 51.8 us  [the longest x6 17.4 us: sparse(): lines = [lax.ppermute(packed[d - 1], 'col', along_y(d)) for d in (1, 2, 3)]]
    ppermute x0 -> x26, waiting for transfers between devices: none -> 44.2 us  [the longest x2 18.2 us: spread_tiles(): p4 = lax.ppermute(p2[HALF:], axes, STEP4)]
    dot_general x8 -> x0, matrix products: 42.9 us -> none  [the longest x4 25.1 us: shards(): jnp.einsum('npx,npy->nxy', high_tiles, right_tiles, preferred_element_typ...]
  transfers between devices with their start and end apart: 5 -> 27, of which waited for: 4 -> 11; matrix products, arithmetic and copies ran while one was open for 20% -> 2% of each run, Pallas kernels for 0% -> 25%
where the time goes in v1:
time: 218 us; the launch traced here: 216 us
  waiting for transfers between devices  66.5 us (31%)
  starting transfers between devices  62.8 us (29%)
  Pallas kernels  61.3 us (28%)
  between operations  15.1 us (7%)
  local copies, waits for them, and re-layouts  6.65 us (3%)
  other arithmetic  3.26 us (1%)
    pallas_call x2, Pallas kernels, sparse(): call(self_kernel, (shape(tiles, F32), shape(tiles, BF)), [SM, SM] + [VM]...  29.6 us
    all_to_all x1, waiting for transfers between devices, sparse(): patterns = lax.all_to_all(named, ('row', 'col'), 0, 0, tiled=True)  22.3 us
    ppermute x2, waiting for transfers between devices, spread_tiles(): p4 = lax.ppermute(p2[HALF:], axes, STEP4)  18.2 us
    ppermute x6, starting transfers between devices, sparse(): lines = [lax.ppermute(packed[d - 1], 'col', along_y(d)) for d in (1, 2, 3)]  17.4 us
    ppermute x3, waiting for transfers between devices, sparse(): arrived = [lax.ppermute(forward[d], 'col', along_y(d)) for d in (1, 2, 3)]  15.4 us
    pallas_call x2, Pallas kernels, sparse(): call(functools.partial(final_kernel, odd), shape(tiles, BF), [SM] * 4 + [...  13.6 us
    all_to_all x1, starting transfers between devices, sparse(): patterns = lax.all_to_all(named, ('row', 'col'), 0, 0, tiled=True)  10.9 us
    ppermute x3, starting transfers between devices, sparse(): lax.ppermute(result, 'row', along_x(d))  7.73 us
  transfers between devices with their start and end apart: 27, of which 11 were waited for; matrix products, arithmetic and copies ran while one was open for 2% of the time, Pallas kernels for 25%

profile of v1, /device:TPU:1, one launch (start us, length us, event | category | flops | bytes accessed | tf_op | source)
XLA Modules:
  0.0 215.6 jit_solution(12277449664234935136)
XLA Ops:
  7.2 4.4 %collective-permute-start.10 = (bf16[23,128,128]{2,1,0:T(8,128)(2,1)}, bf16[23,128,128]{2,1,0:T(8,128)(2,1)S(1)}, u32[]{:S(2)}, u32[]{:S(2)}) collective-permute-start(bf16[23,128,128]{2,1,0:T(8,128)(2,1)} %bitcast.248), channel_id=1, source_target_pairs={{0,4},{1,5},{2,6},{3,7},{8,56},{9,57},{10,58},{11,59},{12,60},{13,... | collective-permute-start | bytes 2261000 | tf_op jit(solution)/shard_map/ppermute | solution.py:420
  11.5 1.9 collective-permute-start.18
  15.9 10.9 %all-to-all-start = ((f32[64,1,128]{2,1,0:T(1,128)}), f32[64,1,128]{2,1,0:T(1,128)S(1)}, u32[]{:S(2)}, u32[]{:S(2)}) async-start(f32[64,1,128]{2,1,0:T(1,128)} %broadcast_in_dim.66), calls=%async_computation.2 | async-start | bytes 65536 | tf_op jit(solution)/shard_map/all_to_all | solution.py:444
  27.5 22.3 %all-to-all-done = f32[64,1,128]{2,1,0:T(1,128)S(1)} async-done(((f32[64,1,128]{2,1,0:T(1,128)}), f32[64,1,128]{2,1,0:T(1,128)S(1)}, u32[]{:S(2)}, u32[]{:S(2)}) %all-to-all-start) | async-done | bytes 32800 | tf_op jit(solution)/shard_map/all_to_all | solution.py:444
  50.4 4.6 %plan.1 = (s32[8,128]{1,0:T(8,128)}, bf16[2,272,128]{2,1,0:T(8,128)(2,1)}) custom-call(s32[4]{0:T(128)} %pad_add_fusion.where, s32[4,23]{1,0:T(4,128)} %bitcast.277, f32[64,128]{1,0:T(8,128)} %bitcast.281, bf16[23,128,128]{2,1,0:T(8,128)(2,1)} %bitcast.249, bf16[23,128,128]{2,1,0:T(8,128)(2,1)} %bitcast.260), custom_call_target="tpu_custom_call" | custom-call | tf_op jit(solution)/shard_map/plan/pallas_call | solution.py:448
  56.5 2.0 collective-permute-start.2
  58.5 2.6 %collective-permute-done.e1 = bf16[2,272,128]{2,1,0:T(8,128)(2,1)S(1)} collective-permute-done((bf16[2,272,128]{2,1,0:T(8,128)(2,1)}, bf16[2,272,128]{2,1,0:T(8,128)(2,1)S(1)}, u32[]{:S(2)}, u32[]{:S(2)}) %collective-permute-start) | collective-permute-done | bytes 139296 | tf_op jit(solution)/shard_map/ppermute | solution.py:451
  61.0 1.9 collective-permute-start.11
  63.0 2.3 %collective-permute-start.19 = (bf16[23,128,128]{2,1,0:T(8,128)(2,1)}, bf16[23,128,128]{2,1,0:T(8,128)(2,1)S(1)}, u32[]{:S(2)}, u32[]{:S(2)}) collective-permute-start(bf16[23,128,128]{2,1,0:T(8,128)(2,1)} %bitcast.261), channel_id=1, source_target_pairs={{0,12},{1,13},{2,14},{3,15},{4,20},{5,21},{6,22},{7,23},{8,24},{9,... | collective-permute-start | bytes 2261000 | tf_op jit(solution)/shard_map/ppermute | solution.py:421
  66.0 2.4 %forward.1 = (bf16[2,272,128]{2,1,0:T(8,128)(2,1)}, bf16[2,272,128]{2,1,0:T(8,128)(2,1)}, bf16[2,272,128]{2,1,0:T(8,128)(2,1)}, bf16[2,272,128]{2,1,0:T(8,128)(2,1)}) custom-call(s32[4]{0:T(128)} %pad_add_fusion.where, bf16[2,272,128]{2,1,0:T(8,128)(2,1)} %get-tuple-element.43.e0, bf16[2,272,128]{2,1,0:T(8,128)(2,1)} %copy-done.33, ...), custom_call_target="tpu_custom_call" | custom-call | tf_op jit(solution)/shard_map/forward/pallas_call | solution.py:452
  68.8 5.2 %collective-permute-done.3.e1 = bf16[2,272,128]{2,1,0:T(8,128)(2,1)S(1)} collective-permute-done((bf16[2,272,128]{2,1,0:T(8,128)(2,1)}, bf16[2,272,128]{2,1,0:T(8,128)(2,1)S(1)}, u32[]{:S(2)}, u32[]{:S(2)}) %collective-permute-start.3) | collective-permute-done | bytes 139296 | tf_op jit(solution)/shard_map/ppermute | solution.py:453
  74.1 5.7 %collective-permute-done.4.e2 = bf16[2,272,128]{2,1,0:T(8,128)(2,1)S(1)} collective-permute-done((bf16[2,272,128]{2,1,0:T(8,128)(2,1)}, bf16[2,272,128]{2,1,0:T(8,128)(2,1)S(1)}, u32[]{:S(2)}, u32[]{:S(2)}) %collective-permute-start.4) | collective-permute-done | bytes 139296 | tf_op jit(solution)/shard_map/ppermute | solution.py:453
  79.8 4.4 %collective-permute-done.5.e3 = bf16[2,272,128]{2,1,0:T(8,128)(2,1)S(1)} collective-permute-done((bf16[2,272,128]{2,1,0:T(8,128)(2,1)}, bf16[2,272,128]{2,1,0:T(8,128)(2,1)S(1)}, u32[]{:S(2)}, u32[]{:S(2)}) %collective-permute-start.5) | collective-permute-done | bytes 139296 | tf_op jit(solution)/shard_map/ppermute | solution.py:453
  84.9 2.2 %extra.1 = bf16[2,272,128]{2,1,0:T(8,128)(2,1)} custom-call(s32[4]{0:T(128)} %pad_add_fusion.where, s32[4,23]{1,0:T(4,128)} %bitcast.278, bf16[23,128,128]{2,1,0:T(8,128)(2,1)} %bitcast.251, bf16[2,272,128]{2,1,0:T(8,128)(2,1)} %get-tuple-element.44.e0, bf16[2,272,128]{2,1,0:T(8,128)(2,1)} %copy-done.36, bf16[2,272,128]{2,1,0:T(8,128)(2,1)} %copy-done.37, ...), custom_call_target="tpu_custom_call" | custom-call | tf_op jit(solution)/shard_map/extra/pallas_call | solution.py:454
  88.5 4.4 %collective-permute-start.7 = (bf16[2,272,128]{2,1,0:T(8,128)(2,1)}, bf16[2,272,128]{2,1,0:T(8,128)(2,1)S(1)}, u32[]{:S(2)}, u32[]{:S(2)}) collective-permute-start(bf16[2,272,128]{2,1,0:T(8,128)(2,1)} %extra.1), channel_id=1, source_target_pairs={{0,32},{16,48},{32,0},{48,16},{1,33},{17,49},{33,1},{49,17},{2,34}... | collective-permute-start | bytes 417800 | tf_op jit(solution)/shard_map/ppermute | solution.py:457
  92.9 2.0 collective-permute-start.8
  94.9 3.6 %collective-permute-done.6 = bf16[2,272,128]{2,1,0:T(8,128)(2,1)S(1)} collective-permute-done((bf16[2,272,128]{2,1,0:T(8,128)(2,1)}, bf16[2,272,128]{2,1,0:T(8,128)(2,1)S(1)}, u32[]{:S(2)}, u32[]{:S(2)}) %collective-permute-start.6) | collective-permute-done | bytes 139296 | tf_op jit(solution)/shard_map/ppermute | solution.py:457
  99.8 2.3 %collective-permute-done.7 = bf16[2,272,128]{2,1,0:T(8,128)(2,1)S(1)} collective-permute-done((bf16[2,272,128]{2,1,0:T(8,128)(2,1)}, bf16[2,272,128]{2,1,0:T(8,128)(2,1)S(1)}, u32[]{:S(2)}, u32[]{:S(2)}) %collective-permute-start.7) | collective-permute-done | bytes 139296 | tf_op jit(solution)/shard_map/ppermute | solution.py:457
  104.4 5.9 %collective-permute-start.9 = (bf16[8,272,128]{2,1,0:T(8,128)(2,1)S(1)}, bf16[8,272,128]{2,1,0:T(8,128)(2,1)S(1)}, u32[]{:S(2)}, u32[]{:S(2)}) collective-permute-start(bf16[8,272,128]{2,1,0:T(8,128)(2,1)S(1)} %pad_maximum_fusion.here), channel_id=1, source_target_pairs={{0,64},{64,0},{1,65},{65,1},{2,66},{66,2},{3,67},{67,3},{4,68},{68... | collective-permute-start | bytes 1671176 | tf_op jit(solution)/shard_map/ppermute | solution.py:458
  113.0 10.5 %collective-permute-done.13.p4.r4 = bf16[11,128,128]{2,1,0:T(8,128)(2,1)S(1)} collective-permute-done((bf16[11,128,128]{2,1,0:T(8,128)(2,1)S(1)}, bf16[11,128,128]{2,1,0:T(8,128)(2,1)S(1)}, u32[]{:S(2)}, u32[]{:S(2)}) %collective-permute-start.13) | collective-permute-done | bytes 360480 | tf_op jit(solution)/shard_map/ppermute | solution.py:423
  123.5 7.7 %collective-permute-done.21.p4 = bf16[11,128,128]{2,1,0:T(8,128)(2,1)S(1)} collective-permute-done((bf16[11,128,128]{2,1,0:T(8,128)(2,1)S(1)}, bf16[11,128,128]{2,1,0:T(8,128)(2,1)S(1)}, u32[]{:S(2)}, u32[]{:S(2)}) %collective-permute-start.21) | collective-permute-done | bytes 360480 | tf_op jit(solution)/shard_map/ppermute | solution.py:423
  132.3 14.7 %squares.3 = (f32[23,128,128]{2,1,0:T(8,128)}, bf16[23,128,128]{2,1,0:T(8,128)(2,1)}) custom-call(s32[4]{0:T(128)} %pad_add_fusion.where, s32[8,128]{1,0:T(8,128)} %get-tuple-element.48.table, bf16[23,128,128]{2,1,0:T(8,128)(2,1)S(1)} %bitcast.262, bf16[23,128,128]{2,1,0:T(8,128)(2,1)} %copy-done.12, bf16[23,128,128]{2,1,0:T(8,128)(2,1)} %copy-done.13, ...), custom_call_target="tpu_custom_call" | custom-call | tf_op jit(solution)/shard_map/squares/pallas_call | solution.py:468
  148.0 14.9 %squares.2 = (f32[23,128,128]{2,1,0:T(8,128)}, bf16[23,128,128]{2,1,0:T(8,128)(2,1)}) custom-call(s32[4]{0:T(128)} %pad_add_fusion.where, s32[8,128]{1,0:T(8,128)} %get-tuple-element.48.table, bf16[23,128,128]{2,1,0:T(8,128)(2,1)S(1)} %bitcast.253, bf16[23,128,128]{2,1,0:T(8,128)(2,1)} %copy-done.7, bf16[23,128,128]{2,1,0:T(8,128)(2,1)} %copy-done.8, ...), custom_call_target="tpu_custom_call" | custom-call | tf_op jit(solution)/shard_map/squares/pallas_call | solution.py:468
  163.2 3.5 %pack.3 = (bf16[9,128,128]{2,1,0:T(8,128)(2,1)}, bf16[9,128,128]{2,1,0:T(8,128)(2,1)}, bf16[9,128,128]{2,1,0:T(8,128)(2,1)}) custom-call(s32[4]{0:T(128)} %pad_add_fusion.where, s32[8,128]{1,0:T(8,128)} %get-tuple-element.48.table, bf16[23,128,128]{2,1,0:T(8,128)(2,1)S(1)} %bitcast.263, bf16[23,128,128]{2,1,0:T(8,128)(2,1)} %copy-done.12, ...), custom_call_target="tpu_custom_call" | custom-call | tf_op jit(solution)/shard_map/pack/pallas_call | solution.py:464
  167.7 4.4 %collective-permute-start.23 = (bf16[9,128,128]{2,1,0:T(8,128)(2,1)}, bf16[9,128,128]{2,1,0:T(8,128)(2,1)S(1)}, u32[]{:S(2)}, u32[]{:S(2)}) collective-permute-start(bf16[9,128,128]{2,1,0:T(8,128)(2,1)} %get-tuple-element.55), channel_id=1, source_target_pairs={{0,2},{1,3},{2,0},{3,1},{4,6},{5,7},{6,4},{7,5},{8,10},{9,11},{10,... | collective-permute-start | bytes 884744 | tf_op jit(solution)/shard_map/ppermute | solution.py:467
  172.1 2.1 collective-permute-start.24
  174.2 3.5 %pack.2 = (bf16[9,128,128]{2,1,0:T(8,128)(2,1)}, bf16[9,128,128]{2,1,0:T(8,128)(2,1)}, bf16[9,128,128]{2,1,0:T(8,128)(2,1)}) custom-call(s32[4]{0:T(128)} %pad_add_fusion.where, s32[8,128]{1,0:T(8,128)} %get-tuple-element.48.table, bf16[23,128,128]{2,1,0:T(8,128)(2,1)S(1)} %bitcast.255, bf16[23,128,128]{2,1,0:T(8,128)(2,1)} %copy-done.7, ...), custom_call_target="tpu_custom_call" | custom-call | tf_op jit(solution)/shard_map/pack/pallas_call | solution.py:464
  177.6 6.7 %collective-permute-start.14 = (bf16[9,128,128]{2,1,0:T(8,128)(2,1)}, bf16[9,128,128]{2,1,0:T(8,128)(2,1)S(1)}, u32[]{:S(2)}, u32[]{:S(2)}) collective-permute-start(bf16[9,128,128]{2,1,0:T(8,128)(2,1)} %get-tuple-element.49), channel_id=1, source_target_pairs={{0,1},{1,2},{2,3},{3,0},{4,5},{5,6},{6,7},{7,4},{8,9},{9,10},{10,1... | collective-permute-start | bytes 884744 | tf_op jit(solution)/shard_map/ppermute | solution.py:467
  186.9 2.0 collective-permute-start.16
  188.9 1.9 flag.1
  192.3 6.2 %finish.3 = bf16[23,128,128]{2,1,0:T(8,128)(2,1)S(1)} custom-call(s32[4]{0:T(128)} %pad_add_fusion.where, s32[4,23]{1,0:T(4,128)S(1)} %bitcast.279, s32[96]{0:T(128)S(1)} %copy-done, s32[8,128]{1,0:T(8,128)} %get-tuple-element.48.table, bf16[23,128,128]{2,1,0:T(8,128)(2,1)S(1)} %bitcast.256, bf16[23,128,128]{2,1,0:T(8,128)(2,1)S(1)} %bitcast.264, ...), custom_call_target="tpu_custom_call" | custom-call | tf_op jit(solution)/shard_map/finish/pallas_call | solution.py:477
  200.5 7.4 %finish.2 = bf16[23,128,128]{2,1,0:T(8,128)(2,1)} custom-call(s32[4]{0:T(128)} %pad_add_fusion.where, s32[4,23]{1,0:T(4,128)S(1)} %bitcast.280, s32[96]{0:T(128)S(1)} %copy-done, s32[8,128]{1,0:T(8,128)} %get-tuple-element.48.table, bf16[23,128,128]{2,1,0:T(8,128)(2,1)S(1)} %bitcast.257, bf16[23,128,128]{2,1,0:T(8,128)(2,1)S(1)} %bitcast.258, ...), custom_call_target="tpu_custom_call" | custom-call | tf_op jit(solution)/shard_map/finish/pallas_call | solution.py:477
  (111 shorter events, 24.0 us)
Async XLA Ops:
  7.2 81.3 %collective-permute-start.10 = (bf16[23,128,128]{2,1,0:T(8,128)(2,1)}, bf16[23,128,128]{2,1,0:T(8,128)(2,1)S(1)}, u32[]{:S(2)}, u32[]{:S(2)}) collective-permute-start(bf16[23,128,128]{2,1,0:T(8,128)(2,1)} %bitcast.248), channel_id=1, source_target_pairs={{0,4},{1,5},{2,6},{3,7},{8,56},{9,57},{10,58},{11,59},{12,60},{13,... | collective-permute-start | bytes 2261000 | tf_op jit(solution)/shard_map/ppermute | solution.py:420
  11.5 81.3 %collective-permute-start.18 = (bf16[23,128,128]{2,1,0:T(8,128)(2,1)}, bf16[23,128,128]{2,1,0:T(8,128)(2,1)S(1)}, u32[]{:S(2)}, u32[]{:S(2)}) collective-permute-start(bf16[23,128,128]{2,1,0:T(8,128)(2,1)} %bitcast.259), channel_id=1, source_target_pairs={{0,4},{1,5},{2,6},{3,7},{8,56},{9,57},{10,58},{11,59},{12,60},{13,... | collective-permute-start | bytes 2261000 | tf_op jit(solution)/shard_map/ppermute | solution.py:420
  15.9 33.9 %all-to-all-start = ((f32[64,1,128]{2,1,0:T(1,128)}), f32[64,1,128]{2,1,0:T(1,128)S(1)}, u32[]{:S(2)}, u32[]{:S(2)}) async-start(f32[64,1,128]{2,1,0:T(1,128)} %broadcast_in_dim.66), calls=%async_computation.2 | async-start | bytes 65536 | tf_op jit(solution)/shard_map/all_to_all | solution.py:444
  55.0 77.3 %copy-start.2 = (bf16[1,1,23,128,128]{4,3,2,1,0:T(8,128)(2,1)S(1)}, bf16[1,1,23,128,128]{4,3,2,1,0:T(8,128)(2,1)}, u32[]{:S(2)}) copy-start(bf16[1,1,23,128,128]{4,3,2,1,0:T(8,128)(2,1)} %param.8) | copy-start | bytes 2260996
  55.0 77.3 %copy-start.9 = (bf16[1,1,23,128,128]{4,3,2,1,0:T(8,128)(2,1)S(1)}, bf16[1,1,23,128,128]{4,3,2,1,0:T(8,128)(2,1)}, u32[]{:S(2)}) copy-start(bf16[1,1,23,128,128]{4,3,2,1,0:T(8,128)(2,1)} %param.9) | copy-start | bytes 2260996
  55.0 6.1 %collective-permute-start = (bf16[2,272,128]{2,1,0:T(8,128)(2,1)}, bf16[2,272,128]{2,1,0:T(8,128)(2,1)S(1)}, u32[]{:S(2)}, u32[]{:S(2)}) collective-permute-start(bf16[2,272,128]{2,1,0:T(8,128)(2,1)} %get-tuple-element.43.e0), channel_id=1, source_target_pairs={{0,4},{1,5},{2,6},{3,7},{4,8},{5,9},{6,10},{7,11},{8,12},{9,13},{1... | collective-permute-start | bytes 417800 | tf_op jit(solution)/shard_map/ppermute | solution.py:451
  55.7 7.3 %collective-permute-start.1 = (bf16[2,272,128]{2,1,0:T(8,128)(2,1)}, bf16[2,272,128]{2,1,0:T(8,128)(2,1)S(1)}, u32[]{:S(2)}, u32[]{:S(2)}) collective-permute-start(bf16[2,272,128]{2,1,0:T(8,128)(2,1)} %get-tuple-element.43.e0), channel_id=1, source_target_pairs={{0,8},{1,9},{2,10},{3,11},{4,12},{5,13},{6,14},{7,15},{8,0},{9,1},... | collective-permute-start | bytes 417800 | tf_op jit(solution)/shard_map/ppermute | solution.py:451
  56.5 8.8 %collective-permute-start.2 = (bf16[2,272,128]{2,1,0:T(8,128)(2,1)}, bf16[2,272,128]{2,1,0:T(8,128)(2,1)S(1)}, u32[]{:S(2)}, u32[]{:S(2)}) collective-permute-start(bf16[2,272,128]{2,1,0:T(8,128)(2,1)} %get-tuple-element.43.e0), channel_id=1, source_target_pairs={{0,12},{1,13},{2,14},{3,15},{4,0},{5,1},{6,2},{7,3},{8,4},{9,5},{1... | collective-permute-start | bytes 417800 | tf_op jit(solution)/shard_map/ppermute | solution.py:451
  61.0 49.3 %collective-permute-start.11 = (bf16[23,128,128]{2,1,0:T(8,128)(2,1)}, bf16[23,128,128]{2,1,0:T(8,128)(2,1)S(1)}, u32[]{:S(2)}, u32[]{:S(2)}) collective-permute-start(bf16[23,128,128]{2,1,0:T(8,128)(2,1)} %bitcast.250), channel_id=1, source_target_pairs={{0,12},{1,13},{2,14},{3,15},{4,20},{5,21},{6,22},{7,23},{8,24},{9,... | collective-permute-start | bytes 2261000 | tf_op jit(solution)/shard_map/ppermute | solution.py:421
  63.0 48.7 %collective-permute-start.19 = (bf16[23,128,128]{2,1,0:T(8,128)(2,1)}, bf16[23,128,128]{2,1,0:T(8,128)(2,1)S(1)}, u32[]{:S(2)}, u32[]{:S(2)}) collective-permute-start(bf16[23,128,128]{2,1,0:T(8,128)(2,1)} %bitcast.261), channel_id=1, source_target_pairs={{0,12},{1,13},{2,14},{3,15},{4,20},{5,21},{6,22},{7,23},{8,24},{9,... | collective-permute-start | bytes 2261000 | tf_op jit(solution)/shard_map/ppermute | solution.py:421
  68.4 5.6 %collective-permute-start.3 = (bf16[2,272,128]{2,1,0:T(8,128)(2,1)}, bf16[2,272,128]{2,1,0:T(8,128)(2,1)S(1)}, u32[]{:S(2)}, u32[]{:S(2)}) collective-permute-start(bf16[2,272,128]{2,1,0:T(8,128)(2,1)} %get-tuple-element.45), channel_id=1, source_target_pairs={{0,1},{1,2},{2,3},{3,0},{4,5},{5,6},{6,7},{7,4},{8,9},{9,10},{10,1... | collective-permute-start | bytes 417800 | tf_op jit(solution)/shard_map/ppermute | solution.py:453
  74.1 5.7 %collective-permute-start.4 = (bf16[2,272,128]{2,1,0:T(8,128)(2,1)}, bf16[2,272,128]{2,1,0:T(8,128)(2,1)S(1)}, u32[]{:S(2)}, u32[]{:S(2)}) collective-permute-start(bf16[2,272,128]{2,1,0:T(8,128)(2,1)} %get-tuple-element.46), channel_id=1, source_target_pairs={{0,2},{1,3},{2,0},{3,1},{4,6},{5,7},{6,4},{7,5},{8,10},{9,11},{10,... | collective-permute-start | bytes 417800 | tf_op jit(solution)/shard_map/ppermute | solution.py:453
  79.8 4.4 %collective-permute-start.5 = (bf16[2,272,128]{2,1,0:T(8,128)(2,1)}, bf16[2,272,128]{2,1,0:T(8,128)(2,1)S(1)}, u32[]{:S(2)}, u32[]{:S(2)}) collective-permute-start(bf16[2,272,128]{2,1,0:T(8,128)(2,1)} %get-tuple-element.47), channel_id=1, source_target_pairs={{0,3},{1,0},{2,1},{3,2},{4,7},{5,4},{6,5},{7,6},{8,11},{9,8},{10,9... | collective-permute-start | bytes 417800 | tf_op jit(solution)/shard_map/ppermute | solution.py:453
  87.1 11.4 %collective-permute-start.6 = (bf16[2,272,128]{2,1,0:T(8,128)(2,1)}, bf16[2,272,128]{2,1,0:T(8,128)(2,1)S(1)}, u32[]{:S(2)}, u32[]{:S(2)}) collective-permute-start(bf16[2,272,128]{2,1,0:T(8,128)(2,1)} %extra.1), channel_id=1, source_target_pairs={{0,16},{16,32},{32,48},{48,0},{1,17},{17,33},{33,49},{49,1},{2,18}... | collective-permute-start | bytes 417800 | tf_op jit(solution)/shard_map/ppermute | solution.py:457
  88.5 42.7 %copy-start.7 = (bf16[23,128,128]{2,1,0:T(8,128)(2,1)}, bf16[23,128,128]{2,1,0:T(8,128)(2,1)S(1)}, u32[]{:S(2)}) copy-start(bf16[23,128,128]{2,1,0:T(8,128)(2,1)S(1)} %collective-permute-done.10.p1.r1) | copy-start | bytes 2260996
  88.5 13.6 %collective-permute-start.7 = (bf16[2,272,128]{2,1,0:T(8,128)(2,1)}, bf16[2,272,128]{2,1,0:T(8,128)(2,1)S(1)}, u32[]{:S(2)}, u32[]{:S(2)}) collective-permute-start(bf16[2,272,128]{2,1,0:T(8,128)(2,1)} %extra.1), channel_id=1, source_target_pairs={{0,32},{16,48},{32,0},{48,16},{1,33},{17,49},{33,1},{49,17},{2,34}... | collective-permute-start | bytes 417800 | tf_op jit(solution)/shard_map/ppermute | solution.py:457
  92.9 38.3 %copy-start.12 = (bf16[23,128,128]{2,1,0:T(8,128)(2,1)}, bf16[23,128,128]{2,1,0:T(8,128)(2,1)S(1)}, u32[]{:S(2)}) copy-start(bf16[23,128,128]{2,1,0:T(8,128)(2,1)S(1)} %collective-permute-done.18.p1) | copy-start | bytes 2260996
  92.9 10.5 %collective-permute-start.8 = (bf16[2,272,128]{2,1,0:T(8,128)(2,1)}, bf16[2,272,128]{2,1,0:T(8,128)(2,1)S(1)}, u32[]{:S(2)}, u32[]{:S(2)}) collective-permute-start(bf16[2,272,128]{2,1,0:T(8,128)(2,1)} %extra.1), channel_id=1, source_target_pairs={{0,48},{16,0},{32,16},{48,32},{1,49},{17,1},{33,17},{49,33},{2,50}... | collective-permute-start | bytes 417800 | tf_op jit(solution)/shard_map/ppermute | solution.py:457
  98.5 32.7 %collective-permute-start.12 = (bf16[12,128,128]{2,1,0:T(8,128)(2,1)S(1)}, bf16[12,128,128]{2,1,0:T(8,128)(2,1)S(1)}, u32[]{:S(2)}, u32[]{:S(2)}) collective-permute-start(bf16[12,128,128]{2,1,0:T(8,128)(2,1)S(1)} %slice.141), channel_id=1, source_target_pairs={{4,8},{5,9},{6,10},{7,11},{12,60},{13,61},{14,62},{15,63},{16,0},{... | collective-permute-start | bytes 1179656 | tf_op jit(solution)/shard_map/ppermute | solution.py:422
  102.1 29.1 %collective-permute-start.20 = (bf16[12,128,128]{2,1,0:T(8,128)(2,1)S(1)}, bf16[12,128,128]{2,1,0:T(8,128)(2,1)S(1)}, u32[]{:S(2)}, u32[]{:S(2)}) collective-permute-start(bf16[12,128,128]{2,1,0:T(8,128)(2,1)S(1)} %slice.143), channel_id=1, source_target_pairs={{4,8},{5,9},{6,10},{7,11},{12,60},{13,61},{14,62},{15,63},{16,0},{... | collective-permute-start | bytes 1179656 | tf_op jit(solution)/shard_map/ppermute | solution.py:422
  104.4 42.6 %copy-start.15 = (bf16[8,272,128]{2,1,0:T(8,128)(2,1)}, bf16[8,272,128]{2,1,0:T(8,128)(2,1)S(1)}, u32[]{:S(2)}) copy-start(bf16[8,272,128]{2,1,0:T(8,128)(2,1)S(1)} %pad_maximum_fusion.here) | copy-start | bytes 1671172
  104.4 67.7 %collective-permute-start.9 = (bf16[8,272,128]{2,1,0:T(8,128)(2,1)S(1)}, bf16[8,272,128]{2,1,0:T(8,128)(2,1)S(1)}, u32[]{:S(2)}, u32[]{:S(2)}) collective-permute-start(bf16[8,272,128]{2,1,0:T(8,128)(2,1)S(1)} %pad_maximum_fusion.here), channel_id=1, source_target_pairs={{0,64},{64,0},{1,65},{65,1},{2,66},{66,2},{3,67},{67,3},{4,68},{68... | collective-permute-start | bytes 1671176 | tf_op jit(solution)/shard_map/ppermute | solution.py:458
  110.3 13.1 %collective-permute-start.13 = (bf16[11,128,128]{2,1,0:T(8,128)(2,1)S(1)}, bf16[11,128,128]{2,1,0:T(8,128)(2,1)S(1)}, u32[]{:S(2)}, u32[]{:S(2)}) collective-permute-start(bf16[11,128,128]{2,1,0:T(8,128)(2,1)S(1)} %slice.142), channel_id=1, source_target_pairs={{4,20},{5,21},{6,22},{7,23},{12,8},{13,9},{14,10},{15,11},{16,28},... | collective-permute-start | bytes 1081352 | tf_op jit(solution)/shard_map/ppermute | solution.py:423
  111.7 19.5 %collective-permute-start.21 = (bf16[11,128,128]{2,1,0:T(8,128)(2,1)S(1)}, bf16[11,128,128]{2,1,0:T(8,128)(2,1)S(1)}, u32[]{:S(2)}, u32[]{:S(2)}) collective-permute-start(bf16[11,128,128]{2,1,0:T(8,128)(2,1)S(1)} %slice.144), channel_id=1, source_target_pairs={{4,20},{5,21},{6,22},{7,23},{12,8},{13,9},{14,10},{15,11},{16,28},... | collective-permute-start | bytes 1081352 | tf_op jit(solution)/shard_map/ppermute | solution.py:423
  147.0 44.5 %collective-permute-start.25 = (bf16[23,128,128]{2,1,0:T(8,128)(2,1)}, bf16[23,128,128]{2,1,0:T(8,128)(2,1)S(1)}, u32[]{:S(2)}, u32[]{:S(2)}) collective-permute-start(bf16[23,128,128]{2,1,0:T(8,128)(2,1)} %get-tuple-element.58), channel_id=1, source_target_pairs={{0,64},{64,0},{1,65},{65,1},{2,66},{66,2},{3,67},{67,3},{4,68},{68... | collective-permute-start | bytes 2261000 | tf_op jit(solution)/shard_map/ppermute | solution.py:475
  162.9 36.5 %collective-permute-start.17 = (bf16[23,128,128]{2,1,0:T(8,128)(2,1)}, bf16[23,128,128]{2,1,0:T(8,128)(2,1)S(1)}, u32[]{:S(2)}, u32[]{:S(2)}) collective-permute-start(bf16[23,128,128]{2,1,0:T(8,128)(2,1)} %get-tuple-element.53), channel_id=1, source_target_pairs={{0,64},{64,0},{1,65},{65,1},{2,66},{66,2},{3,67},{67,3},{4,68},{68... | collective-permute-start | bytes 2261000 | tf_op jit(solution)/shard_map/ppermute | solution.py:475
  166.7 11.0 %collective-permute-start.22 = (bf16[9,128,128]{2,1,0:T(8,128)(2,1)}, bf16[9,128,128]{2,1,0:T(8,128)(2,1)S(1)}, u32[]{:S(2)}, u32[]{:S(2)}) collective-permute-start(bf16[9,128,128]{2,1,0:T(8,128)(2,1)} %get-tuple-element.54), channel_id=1, source_target_pairs={{0,1},{1,2},{2,3},{3,0},{4,5},{5,6},{6,7},{7,4},{8,9},{9,10},{10,1... | collective-permute-start | bytes 884744 | tf_op jit(solution)/shard_map/ppermute | solution.py:467
  167.7 18.0 %collective-permute-start.23 = (bf16[9,128,128]{2,1,0:T(8,128)(2,1)}, bf16[9,128,128]{2,1,0:T(8,128)(2,1)S(1)}, u32[]{:S(2)}, u32[]{:S(2)}) collective-permute-start(bf16[9,128,128]{2,1,0:T(8,128)(2,1)} %get-tuple-element.55), channel_id=1, source_target_pairs={{0,2},{1,3},{2,0},{3,1},{4,6},{5,7},{6,4},{7,5},{8,10},{9,11},{10,... | collective-permute-start | bytes 884744 | tf_op jit(solution)/shard_map/ppermute | solution.py:467
  172.1 14.8 %collective-permute-start.24 = (bf16[9,128,128]{2,1,0:T(8,128)(2,1)}, bf16[9,128,128]{2,1,0:T(8,128)(2,1)S(1)}, u32[]{:S(2)}, u32[]{:S(2)}) collective-permute-start(bf16[9,128,128]{2,1,0:T(8,128)(2,1)} %get-tuple-element.56), channel_id=1, source_target_pairs={{0,3},{1,0},{2,1},{3,2},{4,7},{5,4},{6,5},{7,6},{8,11},{9,8},{10,9... | collective-permute-start | bytes 884744 | tf_op jit(solution)/shard_map/ppermute | solution.py:467
  177.6 20.9 %collective-permute-start.14 = (bf16[9,128,128]{2,1,0:T(8,128)(2,1)}, bf16[9,128,128]{2,1,0:T(8,128)(2,1)S(1)}, u32[]{:S(2)}, u32[]{:S(2)}) collective-permute-start(bf16[9,128,128]{2,1,0:T(8,128)(2,1)} %get-tuple-element.49), channel_id=1, source_target_pairs={{0,1},{1,2},{2,3},{3,0},{4,5},{5,6},{6,7},{7,4},{8,9},{9,10},{10,1... | collective-permute-start | bytes 884744 | tf_op jit(solution)/shard_map/ppermute | solution.py:467
  185.7 13.7 %collective-permute-start.15 = (bf16[9,128,128]{2,1,0:T(8,128)(2,1)}, bf16[9,128,128]{2,1,0:T(8,128)(2,1)S(1)}, u32[]{:S(2)}, u32[]{:S(2)}) collective-permute-start(bf16[9,128,128]{2,1,0:T(8,128)(2,1)} %get-tuple-element.50), channel_id=1, source_target_pairs={{0,2},{1,3},{2,0},{3,1},{4,6},{5,7},{6,4},{7,5},{8,10},{9,11},{10,... | collective-permute-start | bytes 884744 | tf_op jit(solution)/shard_map/ppermute | solution.py:467
  186.9 12.5 %collective-permute-start.16 = (bf16[9,128,128]{2,1,0:T(8,128)(2,1)}, bf16[9,128,128]{2,1,0:T(8,128)(2,1)S(1)}, u32[]{:S(2)}, u32[]{:S(2)}) collective-permute-start(bf16[9,128,128]{2,1,0:T(8,128)(2,1)} %get-tuple-element.51), channel_id=1, source_target_pairs={{0,3},{1,0},{2,1},{3,2},{4,7},{5,4},{6,5},{7,6},{8,11},{9,8},{10,9... | collective-permute-start | bytes 884744 | tf_op jit(solution)/shard_map/ppermute | solution.py:467
  (26 other events, 208.8 us)
